TPU v7x, 32 devices: a whole 2x2x4 slice. The times are simulated.
32 devices in a mesh: ctx: 8 (over y, x, core), exp: 4 (over z).
Axes of the slice: x: 2, y: 2, z: 4, core: 2. Of those that a mesh axis runs over, the one named last changes fastest.
Arguments:
- inputs: bfloat16 [1024, 1024], P('exp', 'ctx'), may hold values from -6 to 6
- conv_taps: float32 [1024, 31], P('exp'), may hold values from -1 to 1
- norm_gain: bfloat16 [1024], P('exp'), may hold values from 0.099609375 to 1.8984375
- routes: int32 [1024, 2], P('ctx'), may hold values from 0 to 7, all different within a row; in each aligned block of 128 rows (0 to 127, 128 to 255, ...) at most 32 rows name the same one
- gate_probs: float32 [1024, 2], P('ctx'), may hold values from 0.1 to 0.9
- w_gate: bfloat16 [8, 1024, 4096], P('ctx', None, 'exp'), may hold values from -0.1875 to 0.1875
- w_up: bfloat16 [8, 1024, 4096], P('ctx', None, 'exp'), may hold values from -0.1875 to 0.1875
- w_down: bfloat16 [8, 4096, 1024], P('ctx', 'exp'), may hold values from -0.09375 to 0.09375
- grad_out: bfloat16 [1024, 1024], P('exp', 'ctx'), may hold values from -6 to 6
Outputs:
- layer_out: bfloat16 [1024, 1024], P('exp', 'ctx')
- grad_inputs: bfloat16 [1024, 1024], P('exp', 'ctx')
- grad_taps: float32 [1024, 31], P('exp')
- grad_gain: float32 [1024], P('exp')
- grad_gates: float32 [1024, 2], P('ctx')
- grad_w_gate: bfloat16 [8, 1024, 4096], P('ctx', None, 'exp')
- grad_w_up: bfloat16 [8, 1024, 4096], P('ctx', None, 'exp')
- grad_w_down: bfloat16 [8, 4096, 1024], P('ctx', 'exp')
Inputs may be any that keep to these rules, and one draw needn't show every extreme that they name: `routes`: in each aligned block of 128 rows (the rows of one index of ctx) no expert is named by more than 32 rows, a bound that some block reaches; the two experts of a row differ.
All inputs are finite; a program needn't handle non-finite values.
Results may differ from a plain program's by a relative error of at most 0.025.
Values may be sent and summed in bfloat16 or wider, within the bound.
A program may use at most 64 MiB of HBM per device.

v0:
```python
import jax
import jax.numpy as jnp
from jax import lax
from jax.sharding import PartitionSpec as P

EPS = 1e-05


def padded_2(cells, sides, width):
    for axis, dim in sides:
        count = lax.axis_size(axis)
        head = lax.slice_in_dim(cells, 0, width, axis=dim)
        tail = lax.slice_in_dim(cells, cells.shape[dim] - width, cells.shape[dim], axis=dim)
        cells = jnp.concatenate(
            [
                lax.ppermute(tail, axis, [(i, (i + 1) % count) for i in range(count)]),
                cells,
                lax.ppermute(head, axis, [((i + 1) % count, i) for i in range(count)]),
            ],
            axis=dim,
        )
    return cells


def shortened(x):

    def short(part):
        return part.astype(jnp.bfloat16) if part.dtype == jnp.float32 else part

    return jax.tree.map(short, x)


def slot_rows(routes, experts, capacity):
    flat = routes.reshape(-1)
    onehot = (flat[:, None] == jnp.arange(experts, dtype=jnp.int32)[None, :]).astype(jnp.int32)
    before = jnp.cumsum(onehot, axis=0, dtype=jnp.int32) - onehot
    place = jnp.sum(before * onehot, axis=1, dtype=jnp.int32)
    return flat * capacity + place


def bring_back(values, dest, weights, experts, capacity, whole_cot):
    width = values.shape[1]
    back = lax.all_to_all(
        values.reshape(experts, capacity, width).astype(jnp.bfloat16),
        "ctx",
        split_axis=0,
        concat_axis=0,
        tiled=True,
    ).astype(jnp.float32)
    picked = back.reshape(experts * capacity, width)[dest]
    term = jnp.sum((picked * weights[:, None]).reshape(-1, 2, width), axis=1)
    share = lax.psum_scatter(
        term.astype(jnp.bfloat16), "exp", scatter_dimension=1, tiled=True
    ).astype(jnp.float32)
    dots = None if whole_cot is None else jnp.sum(picked * whole_cot, axis=1)
    return (share, dots)


def local(inputs, conv_taps, norm_gain, routes, gate_probs, w_gate, w_up, w_down, grad_out):
    chans, tokens = inputs.shape
    taps = conv_taps.shape[1]
    half = taps // 2
    width = w_gate.shape[1]
    experts = lax.axis_size("ctx")
    capacity = max(tokens // 8, (2 * tokens + experts - 1) // experts)
    padded = padded_2(inputs, (("ctx", 1),), half)
    padded_f = padded.astype(jnp.float32)
    conv = jnp.zeros((chans, tokens), jnp.float32)
    for offset in range(taps):
        conv = conv + conv_taps[:, offset : offset + 1] * padded_f[:, offset : offset + tokens]
    mixed = (inputs.astype(jnp.float32) + conv).astype(jnp.bfloat16)
    mixed_f = mixed.astype(jnp.float32)
    gain_f = norm_gain.astype(jnp.float32)
    squares = lax.psum(jnp.sum(mixed_f * mixed_f, axis=0), "exp")
    scale = lax.rsqrt(squares / width + EPS)
    normed_part = (mixed_f * gain_f[:, None] * scale[None, :]).astype(jnp.bfloat16)
    normed, cotangent = (
        lax.all_gather(normed_part, "exp", axis=0, tiled=True),
        lax.all_gather(grad_out, "exp", axis=0, tiled=True),
    )
    dest = slot_rows(routes, experts, capacity)
    gates = gate_probs.reshape(-1)
    cot_rows = jnp.repeat(cotangent.T, 2, axis=0).astype(jnp.float32)
    token_rows = jnp.repeat(normed.T, 2, axis=0)
    scaled_rows = (cot_rows * gates[:, None]).astype(jnp.bfloat16)
    empty = jnp.zeros((experts * capacity, width), jnp.bfloat16)
    send_x = empty.at[dest].set(token_rows).reshape(experts, capacity, width)
    send_dy = empty.at[dest].set(scaled_rows).reshape(experts, capacity, width)
    recv_x, recv_dy = (
        lax.all_to_all(send_x, "ctx", split_axis=0, concat_axis=0, tiled=True),
        lax.all_to_all(send_dy, "ctx", split_axis=0, concat_axis=0, tiled=True),
    )
    rows_x = recv_x.reshape(-1, width)
    rows_dy = recv_dy.reshape(-1, width)
    weight_gate = w_gate[0]
    weight_up = w_up[0]
    weight_down = w_down[0]
    gate_act = jnp.dot(rows_x, weight_gate, preferred_element_type=jnp.float32)
    up_act = jnp.dot(rows_x, weight_up, preferred_element_type=jnp.float32)
    sigma = jax.nn.sigmoid(gate_act)
    hidden = (gate_act * sigma * up_act).astype(jnp.bfloat16)
    partial_out = jnp.dot(hidden, weight_down, preferred_element_type=jnp.float32)
    moe_share, gate_dots = bring_back(partial_out, dest, gates, experts, capacity, cot_rows)
    layer_out = (mixed_f + moe_share.T).astype(jnp.bfloat16)
    grad_gates = lax.psum(gate_dots, "exp").reshape(tokens, 2)
    contract_last = (((1,), (1,)), ((), ()))
    contract_first = (((0,), (0,)), ((), ()))
    d_hidden = lax.dot_general(
        rows_dy, weight_down, contract_last, preferred_element_type=jnp.float32
    )
    grad_down = lax.dot_general(
        hidden, rows_dy, contract_first, preferred_element_type=jnp.float32
    ).astype(jnp.bfloat16)
    d_gate = (d_hidden * up_act * sigma * (1.0 + gate_act * (1.0 - sigma))).astype(jnp.bfloat16)
    d_up = (d_hidden * gate_act * sigma).astype(jnp.bfloat16)
    grad_gate = lax.dot_general(
        rows_x, d_gate, contract_first, preferred_element_type=jnp.float32
    ).astype(jnp.bfloat16)
    grad_up = lax.dot_general(
        rows_x, d_up, contract_first, preferred_element_type=jnp.float32
    ).astype(jnp.bfloat16)
    d_rows = lax.dot_general(d_gate, weight_gate, contract_last, preferred_element_type=jnp.float32)
    d_rows = d_rows + lax.dot_general(
        d_up, weight_up, contract_last, preferred_element_type=jnp.float32
    )
    d_share, unused_dots = bring_back(d_rows, dest, jnp.ones_like(gates), experts, capacity, None)
    d_normed = d_share.T
    gain_local = jnp.sum(d_normed * mixed_f * scale[None, :], axis=1)
    norm_terms = lax.psum(jnp.sum(d_normed * gain_f[:, None] * mixed_f, axis=0), "exp")
    cot_own = grad_out.astype(jnp.float32)
    d_mixed = (
        cot_own
        + gain_f[:, None] * d_normed * scale[None, :]
        - mixed_f * (norm_terms * scale * scale * scale / width)[None, :]
    )
    grad_padded = padded_2(shortened(d_mixed), (("ctx", 1),), half).astype(d_mixed.dtype)
    grad_in = d_mixed
    tap_parts = []
    for offset in range(taps):
        grad_in = (
            grad_in
            + conv_taps[:, offset : offset + 1]
            * grad_padded[:, 2 * half - offset : 2 * half - offset + tokens]
        )
        tap_parts.append(jnp.sum(d_mixed * padded_f[:, offset : offset + tokens], axis=1))
    tap_local = jnp.stack(tap_parts, axis=1)
    grad_taps, grad_gain = lax.psum((tap_local, gain_local), "ctx")
    return (
        layer_out,
        grad_in.astype(jnp.bfloat16),
        grad_taps,
        grad_gain,
        grad_gates,
        grad_gate[None],
        grad_up[None],
        grad_down[None],
    )


def solution(mesh):
    return jax.shard_map(
        local,
        mesh=mesh,
        in_specs=(
            P("exp", "ctx"),
            P("exp", None),
            P("exp"),
            P("ctx", None),
            P("ctx", None),
            P("ctx", None, "exp"),
            P("ctx", None, "exp"),
            P("ctx", "exp", None),
            P("exp", "ctx"),
        ),
        out_specs=(
            P("exp", "ctx"),
            P("exp", "ctx"),
            P("exp", None),
            P("exp"),
            P("ctx", None),
            P("ctx", None, "exp"),
            P("ctx", None, "exp"),
            P("ctx", "exp", None),
        ),
        check_vma=False,
    )
```

profile of v0, /device:TPU:0, one launch (start us, length us, event | category | flops | bytes accessed | tf_op | source)
XLA Modules:
  0.0 213.7 jit_solution(18306011151170475799)
XLA Ops:
  8.8 2.9 %collective-permute-start.1 = (bf16[256,15]{0,1:T(8,128)(2,1)S(1)}, bf16[256,15]{0,1:T(8,128)(2,1)S(1)}, u32[]{:S(2)}, u32[]{:S(2)}) collective-permute-start(bf16[256,15]{0,1:T(8,128)(2,1)S(1)} %get-tuple-element.72), channel_id=1, source_target_pairs={{4,0},{8,4},{12,8},{16,12},{20,16},{24,20},{28,24},{0,28},{5,1},{9... | collective-permute-start | bytes 23048 | tf_op jit(solution)/shard_map/ppermute | solution.py:18
  15.5 15.0 %all_gather.7 = bf16[1024,128]{1,0:T(8,128)(2,1)S(1)} all-gather(bf16[256,128]{1,0:T(8,128)(2,1)} %param.17), channel_id=1, replica_groups=mesh['ctx'=8,'exp'=4] {'exp'}, dimensions={0}, use_global_device_ids=true | all-gather | bytes 327680 | tf_op jit(solution)/shard_map/all_gather | solution.py:79
  34.2 2.5 %scatter_custom_fusion.1 = bf16[256,1024]{1,0:T(8,128)(2,1)} fusion(s32[256]{0:T(256)S(1)} %bitcast.245, f32[256,1024]{1,0:T(8,128)S(1)} %convert_element_type.108, f32[256]{0:T(256)S(1)} %mul.828, bf16[]{:T(256)} %constant.8.clone.1), kind=kCustom, calls=%fused_computation.29 | custom fusion | flops 524288 | bytes 1573890 | tf_op jit(solution)/shard_map/scatter | solution.py:88
  36.7 4.1 %all-to-all-start.2 = ((bf16[8,32,1024]{2,1,0:T(8,128)(2,1)}), bf16[8,32,1024]{2,1,0:T(8,128)(2,1)}, u32[]{:S(2)}, u32[]{:S(2)}) async-start(bf16[8,32,1024]{2,1,0:T(8,128)(2,1)} %bitcast.149), calls=%async_computation.3 | async-start | bytes 1048576 | tf_op jit(solution)/shard_map/all_to_all | solution.py:91
  42.4 11.9 %psum.35 = f32[128]{0:T(128)S(1)} all-reduce(f32[128]{0:T(128)} %get-tuple-element.62), channel_id=1, replica_groups=mesh['ctx'=8,'exp'=4] {'exp'}, use_global_device_ids=true, to_apply=%region_4.5 | all-reduce | flops 128 | bytes 1024 | tf_op jit(solution)/shard_map/psum | solution.py:74
  54.9 13.8 %all_gather.6 = bf16[1024,128]{0,1:T(8,128)(2,1)S(1)} all-gather(bf16[256,128]{0,1:T(8,128)(2,1)S(1)} %fusion.27), channel_id=1, replica_groups=mesh['ctx'=8,'exp'=4] {'exp'}, dimensions={0}, use_global_device_ids=true | all-gather | bytes 327680 | tf_op jit(solution)/shard_map/all_gather | solution.py:78
  69.2 2.6 %scatter_custom_fusion = bf16[256,1024]{1,0:T(8,128)(2,1)} fusion(s32[256]{0:T(256)} %bitcast.246, bf16[256,1024]{1,0:T(8,128)(2,1)S(1)} %reshape.158, bf16[]{:T(256)} %constant.8.clone.1), kind=kCustom, calls=%fused_computation.41 | custom fusion | bytes 524800 | tf_op jit(solution)/shard_map/scatter | solution.py:87
  71.8 4.1 %all-to-all-start = ((bf16[8,32,1024]{2,1,0:T(8,128)(2,1)}), bf16[8,32,1024]{2,1,0:T(8,128)(2,1)S(1)}, u32[]{:S(2)}, u32[]{:S(2)}) async-start(bf16[8,32,1024]{2,1,0:T(8,128)(2,1)} %bitcast.36), calls=%async_computation | async-start | bytes 1048576 | tf_op jit(solution)/shard_map/all_to_all | solution.py:90
  76.5 3.5 %fusion.2 = f32[256,1024]{1,0:T(8,128)} fusion(bf16[256,1024]{1,0:T(8,128)(2,1)} %bitcast.47, bf16[1,1024,1024]{2,1,0:T(8,128)(2,1)} %param.16), kind=kOutput, calls=%fused_computation.6 | convolution fusion | flops 536870912 | bytes 3670016 | tf_op jit(solution)/shard_map/dot_general | solution.py:108
  80.0 5.6 %all-to-all-done = bf16[8,32,1024]{2,1,0:T(8,128)(2,1)S(1)} async-done(((bf16[8,32,1024]{2,1,0:T(8,128)(2,1)}), bf16[8,32,1024]{2,1,0:T(8,128)(2,1)S(1)}, u32[]{:S(2)}, u32[]{:S(2)}) %all-to-all-start) | async-done | bytes 524320 | tf_op jit(solution)/shard_map/all_to_all | solution.py:90
  85.6 2.5 %fusion.6 = f32[256,1024]{1,0:T(8,128)S(1)} fusion(bf16[256,1024]{1,0:T(8,128)(2,1)S(1)} %bitcast.145, bf16[1,1024,1024]{2,1,0:T(8,128)(2,1)} %param.15), kind=kOutput, calls=%fused_computation.10 | convolution fusion | flops 536870912 | bytes 3670016 | tf_op jit(solution)/shard_map/dot_general | solution.py:99
  92.5 3.5 %all-to-all-start.1 = ((bf16[8,32,1024]{2,1,0:T(8,128)(2,1)}), bf16[8,32,1024]{2,1,0:T(8,128)(2,1)S(1)}, u32[]{:S(2)}, u32[]{:S(2)}) async-start(bf16[8,32,1024]{2,1,0:T(8,128)(2,1)} %fusion.15), calls=%async_computation.1 | async-start | bytes 1048576 | tf_op jit(solution)/shard_map/all_to_all | solution.py:43
  96.0 2.4 %fusion.4 = f32[256,1024]{1,0:T(8,128)S(1)} fusion(bf16[256,1024]{1,0:T(8,128)(2,1)S(1)} %get-tuple-element.66, bf16[1,1024,1024]{2,1,0:T(8,128)(2,1)} %param.15), kind=kOutput, calls=%fused_computation.8 | convolution fusion | flops 536870912 | bytes 3670016 | tf_op jit(solution)/shard_map/dot_general | solution.py:123
  100.0 5.7 %all-to-all-done.1 = bf16[8,32,1024]{2,1,0:T(8,128)(2,1)S(1)} async-done(((bf16[8,32,1024]{2,1,0:T(8,128)(2,1)}), bf16[8,32,1024]{2,1,0:T(8,128)(2,1)S(1)}, u32[]{:S(2)}, u32[]{:S(2)}) %all-to-all-start.1) | async-done | bytes 524320 | tf_op jit(solution)/shard_map/all_to_all | solution.py:43
  105.6 4.2 %all-to-all-start.3 = ((bf16[8,32,1024]{2,1,0:T(8,128)(2,1)}), bf16[8,32,1024]{2,1,0:T(8,128)(2,1)}, u32[]{:S(2)}, u32[]{:S(2)}) async-start(bf16[8,32,1024]{2,1,0:T(8,128)(2,1)} %bitcast.48), calls=%async_computation.4 | async-start | bytes 1048576 | tf_op jit(solution)/shard_map/all_to_all | solution.py:43
  113.3 2.9 %gather.9 = f32[128,2,1024]{2,1,0:T(2,128)} reshape(f32[256,1024]{1,0:T(8,128)} %gather_fusion) | data formatting | bytes 2097152 | tf_op jit(solution)/shard_map/gather | solution.py:50
  116.2 3.3 %multiply_reduce_fusion.1 = bf16[128,1024]{1,0:T(8,128)(2,1)} fusion(f32[128,2,1024]{2,1,0:T(2,128)} %gather.9, f32[128,2]{1,0:T(8,128)S(1)} %copy.35), kind=kLoop, calls=%fused_computation.26 | loop fusion | flops 393216 | bytes 1311744 | tf_op jit(solution)/shard_map/reduce_sum | solution.py:51
  125.0 2.9 %reshape.132 = f32[128,2,1024]{2,1,0:T(2,128)} reshape(f32[256,1024]{1,0:T(8,128)} %gather_fusion.1) | data formatting | bytes 2097152 | tf_op jit(solution)/shard_map/reshape | solution.py:51
  127.9 3.2 %reduce_sum.348 = bf16[128,1024]{1,0:T(8,128)(2,1)} reduce(f32[128,2,1024]{2,1,0:T(2,128)} %reshape.132, f32[]{:T(128)} %constant.7.clone.1), dimensions={1}, to_apply=%region_9.10 | reduce | flops 131072 | bytes 1310724 | tf_op jit(solution)/shard_map/reduce_sum | solution.py:51
  133.2 3.3 %convert_bitcast_fusion = bf16[1,1024,1024]{2,1,0:T(8,128)(2,1)} fusion(bf16[256,1024]{1,0:T(8,128)(2,1)S(1)} %copy-done.15, bf16[256,1024]{1,0:T(8,128)(2,1)} %bitcast.47), kind=kOutput, calls=%fused_computation.16 | convolution fusion | flops 537919488 | bytes 3145728 | tf_op jit(solution)/shard_map/dot_general | solution.py:111
  137.8 20.4 %reduce-scatter.5.cloned.1.call-done = bf16[128,256]{1,0:T(8,128)(2,1)} async-done(((bf16[128,1024]{1,0:T(8,128)(2,1)}), bf16[128,256]{1,0:T(8,128)(2,1)}) %reduce-scatter.5.cloned.1.call-update) | async-done | bytes 65552 | tf_op jit(solution)/shard_map/reduce_scatter | solution.py:52
  159.1 17.2 %all-reduce.1 = (f32[128]{0:T(128)S(1)}, f32[128,2]{1,0:T(8,128)S(1)}) all-reduce(f32[128]{0:T(128)S(1)} %get-tuple-element.56, f32[128,2]{1,0:T(8,128)S(1)} %reshape.133), channel_id=1, replica_groups=mesh['ctx'=8,'exp'=4] {'exp'}, use_global_device_ids=true, to_apply=%region_12.13 | all-reduce | flops 384 | bytes 3072 | tf_op jit(solution)/shard_map/psum | solution.py:129
  178.1 2.6 %collective-permute-start.3 = (bf16[256,15]{0,1:T(8,128)(2,1)S(1)}, bf16[256,15]{0,1:T(8,128)(2,1)S(1)}, u32[]{:S(2)}, u32[]{:S(2)}) collective-permute-start(bf16[256,15]{0,1:T(8,128)(2,1)S(1)} %get-tuple-element.69), channel_id=1, source_target_pairs={{4,0},{8,4},{12,8},{16,12},{20,16},{24,20},{28,24},{0,28},{5,1},{9... | collective-permute-start | bytes 23048 | tf_op jit(solution)/shard_map/ppermute | solution.py:18
  180.8 23.3 %all-reduce = (f32[256,31]{0,1:T(8,128)}, f32[256]{0:T(256)}) all-reduce(f32[256,31]{0,1:T(8,128)S(1)} %stack.127, f32[256]{0:T(256)S(1)} %get-tuple-element.55), channel_id=1, replica_groups=mesh['ctx'=8,'exp'=4] {'ctx'}, use_global_device_ids=true, to_apply=%region_44.45 | all-reduce | flops 8192 | bytes 65536 | tf_op jit(solution)/shard_map/psum | solution.py:147
  (199 shorter events, 35.3 us)
Async XLA Ops:
  7.2 81.0 %copy-start = (bf16[1,1024,1024]{2,1,0:T(8,128)(2,1)S(1)}, bf16[1,1024,1024]{2,1,0:T(8,128)(2,1)}, u32[]{:S(2)}) copy-start(bf16[1,1024,1024]{2,1,0:T(8,128)(2,1)} %param.14) | copy-start | bytes 6291460
  8.3 32.8 %collective-permute-start = (bf16[256,15]{0,1:T(8,128)(2,1)S(1)}, bf16[256,15]{0,1:T(8,128)(2,1)S(1)}, u32[]{:S(2)}, u32[]{:S(2)}) collective-permute-start(bf16[256,15]{0,1:T(8,128)(2,1)S(1)} %get-tuple-element.71), channel_id=1, source_target_pairs={{0,4},{4,8},{8,12},{12,16},{16,20},{20,24},{24,28},{28,0},{1,5},{5... | collective-permute-start | bytes 23048 | tf_op jit(solution)/shard_map/ppermute | solution.py:16
  8.8 32.4 %collective-permute-start.1 = (bf16[256,15]{0,1:T(8,128)(2,1)S(1)}, bf16[256,15]{0,1:T(8,128)(2,1)S(1)}, u32[]{:S(2)}, u32[]{:S(2)}) collective-permute-start(bf16[256,15]{0,1:T(8,128)(2,1)S(1)} %get-tuple-element.72), channel_id=1, source_target_pairs={{4,0},{8,4},{12,8},{16,12},{20,16},{24,20},{28,24},{0,28},{5,1},{9... | collective-permute-start | bytes 23048 | tf_op jit(solution)/shard_map/ppermute | solution.py:18
  36.7 35.1 %all-to-all-start.2 = ((bf16[8,32,1024]{2,1,0:T(8,128)(2,1)}), bf16[8,32,1024]{2,1,0:T(8,128)(2,1)}, u32[]{:S(2)}, u32[]{:S(2)}) async-start(bf16[8,32,1024]{2,1,0:T(8,128)(2,1)} %bitcast.149), calls=%async_computation.3 | async-start | bytes 1048576 | tf_op jit(solution)/shard_map/all_to_all | solution.py:91
  71.8 13.8 %all-to-all-start = ((bf16[8,32,1024]{2,1,0:T(8,128)(2,1)}), bf16[8,32,1024]{2,1,0:T(8,128)(2,1)S(1)}, u32[]{:S(2)}, u32[]{:S(2)}) async-start(bf16[8,32,1024]{2,1,0:T(8,128)(2,1)} %bitcast.36), calls=%async_computation | async-start | bytes 1048576 | tf_op jit(solution)/shard_map/all_to_all | solution.py:90
  92.5 13.2 %all-to-all-start.1 = ((bf16[8,32,1024]{2,1,0:T(8,128)(2,1)}), bf16[8,32,1024]{2,1,0:T(8,128)(2,1)S(1)}, u32[]{:S(2)}, u32[]{:S(2)}) async-start(bf16[8,32,1024]{2,1,0:T(8,128)(2,1)} %fusion.15), calls=%async_computation.1 | async-start | bytes 1048576 | tf_op jit(solution)/shard_map/all_to_all | solution.py:43
  105.6 16.2 %all-to-all-start.3 = ((bf16[8,32,1024]{2,1,0:T(8,128)(2,1)}), bf16[8,32,1024]{2,1,0:T(8,128)(2,1)}, u32[]{:S(2)}, u32[]{:S(2)}) async-start(bf16[8,32,1024]{2,1,0:T(8,128)(2,1)} %bitcast.48), calls=%async_computation.4 | async-start | bytes 1048576 | tf_op jit(solution)/shard_map/all_to_all | solution.py:43
  109.8 27.9 %reduce-scatter.3.cloned.1.call-start = ((), (), s32[]{:S(2)}) async-start(), calls=%async_computation.6 | async-start | bytes 327680 | tf_op jit(solution)/shard_map/reduce_scatter | solution.py:52
  119.6 38.6 %reduce-scatter.5.cloned.1.call-start = ((), (), s32[]{:S(2)}) async-start(), calls=%async_computation.7 | async-start | bytes 327680 | tf_op jit(solution)/shard_map/reduce_scatter | solution.py:52
  133.2 43.1 %copy-start.65 = (f32[128]{0:T(128)S(1)}, f32[128]{0:T(128)}, u32[]{:S(2)}) copy-start(f32[128]{0:T(128)} %copy-done.64) | copy-start | bytes 1540
  176.4 29.1 %copy-start.19 = (f32[256,1]{0,1:T(1,128)S(1)}, f32[256,1]{0,1:T(1,128)}, u32[]{:S(2)}) copy-start(f32[256,1]{0,1:T(1,128)} %copy-done.18) | copy-start | bytes 3076
  176.4 29.1 %copy-start.21 = (f32[256,1]{0,1:T(1,128)S(1)}, f32[256,1]{0,1:T(1,128)}, u32[]{:S(2)}) copy-start(f32[256,1]{0,1:T(1,128)} %copy-done.20) | copy-start | bytes 3076
  176.4 29.1 %copy-start.23 = (f32[256,1]{0,1:T(1,128)S(1)}, f32[256,1]{0,1:T(1,128)}, u32[]{:S(2)}) copy-start(f32[256,1]{0,1:T(1,128)} %copy-done.22) | copy-start | bytes 3076
  176.4 29.1 %copy-start.25 = (f32[256,1]{0,1:T(1,128)S(1)}, f32[256,1]{0,1:T(1,128)}, u32[]{:S(2)}) copy-start(f32[256,1]{0,1:T(1,128)} %copy-done.24) | copy-start | bytes 3076
  176.4 29.1 %copy-start.27 = (f32[256,1]{0,1:T(1,128)S(1)}, f32[256,1]{0,1:T(1,128)}, u32[]{:S(2)}) copy-start(f32[256,1]{0,1:T(1,128)} %copy-done.26) | copy-start | bytes 3076
  176.4 29.1 %copy-start.29 = (f32[256,1]{0,1:T(1,128)S(1)}, f32[256,1]{0,1:T(1,128)}, u32[]{:S(2)}) copy-start(f32[256,1]{0,1:T(1,128)} %copy-done.28) | copy-start | bytes 3076
  176.4 29.1 %copy-start.31 = (f32[256,1]{0,1:T(1,128)S(1)}, f32[256,1]{0,1:T(1,128)}, u32[]{:S(2)}) copy-start(f32[256,1]{0,1:T(1,128)} %copy-done.30) | copy-start | bytes 3076
  176.4 29.1 %copy-start.33 = (f32[256,1]{0,1:T(1,128)S(1)}, f32[256,1]{0,1:T(1,128)}, u32[]{:S(2)}) copy-start(f32[256,1]{0,1:T(1,128)} %copy-done.32) | copy-start | bytes 3076
  176.4 29.1 %copy-start.35 = (f32[256,1]{0,1:T(1,128)S(1)}, f32[256,1]{0,1:T(1,128)}, u32[]{:S(2)}) copy-start(f32[256,1]{0,1:T(1,128)} %copy-done.34) | copy-start | bytes 3076
  176.5 29.1 %copy-start.37 = (f32[256,1]{0,1:T(1,128)S(1)}, f32[256,1]{0,1:T(1,128)}, u32[]{:S(2)}) copy-start(f32[256,1]{0,1:T(1,128)} %copy-done.36) | copy-start | bytes 3076
  176.5 29.1 %copy-start.39 = (f32[256,1]{0,1:T(1,128)S(1)}, f32[256,1]{0,1:T(1,128)}, u32[]{:S(2)}) copy-start(f32[256,1]{0,1:T(1,128)} %copy-done.38) | copy-start | bytes 3076
  176.5 29.1 %copy-start.41 = (f32[256,1]{0,1:T(1,128)S(1)}, f32[256,1]{0,1:T(1,128)}, u32[]{:S(2)}) copy-start(f32[256,1]{0,1:T(1,128)} %copy-done.40) | copy-start | bytes 3076
  178.0 27.5 %collective-permute-start.2 = (bf16[256,15]{0,1:T(8,128)(2,1)S(1)}, bf16[256,15]{0,1:T(8,128)(2,1)S(1)}, u32[]{:S(2)}, u32[]{:S(2)}) collective-permute-start(bf16[256,15]{0,1:T(8,128)(2,1)S(1)} %get-tuple-element.68), channel_id=1, source_target_pairs={{0,4},{4,8},{8,12},{12,16},{16,20},{20,24},{24,28},{28,0},{1,5},{5... | collective-permute-start | bytes 23048 | tf_op jit(solution)/shard_map/ppermute | solution.py:16
  178.1 27.4 %collective-permute-start.3 = (bf16[256,15]{0,1:T(8,128)(2,1)S(1)}, bf16[256,15]{0,1:T(8,128)(2,1)S(1)}, u32[]{:S(2)}, u32[]{:S(2)}) collective-permute-start(bf16[256,15]{0,1:T(8,128)(2,1)S(1)} %get-tuple-element.69), channel_id=1, source_target_pairs={{4,0},{8,4},{12,8},{16,12},{20,16},{24,20},{28,24},{0,28},{5,1},{9... | collective-permute-start | bytes 23048 | tf_op jit(solution)/shard_map/ppermute | solution.py:18
  (52 other events, 427.1 us)
Sparse Core Ops, SparseCore 0:
  119.7 18.0 reduce-scatter.2
  140.1 17.9 reduce-scatter.4
where the time goes:
time: 215 us; the launch traced here: 214 us
  blocking collectives  81.2 us (38%)
  waiting for transfers between devices  32.6 us (15%)
  local copies, waits for them, and re-layouts  24.1 us (11%)
  starting transfers between devices  22.3 us (10%)
  matrix products  20.8 us (10%)
  other arithmetic  17.6 us (8%)
  between operations  15.1 us (7%)
    psum x1, blocking collectives, local(): grad_taps, grad_gain = lax.psum((tap_local, gain_local), 'ctx')  23.3 us
    reduce_scatter x2, waiting for transfers between devices, bring_back(): lax.psum_scatter(term.astype(jnp.bfloat16), 'exp', scatter_dimension=1, t...  21.3 us
    psum x1, blocking collectives, local(): lax.psum(jnp.sum(d_normed * gain_f[:, None] * mixed_f, axis=0), 'exp')  17.2 us
    all_gather x1, blocking collectives, local(): lax.all_gather(grad_out, 'exp', axis=0, tiled=True)  15 us
    all_gather x1, blocking collectives, local(): lax.all_gather(normed_part, 'exp', axis=0, tiled=True)  13.8 us
    psum x1, blocking collectives, local(): squares = lax.psum(jnp.sum(mixed_f * mixed_f, axis=0), 'exp')  11.9 us
    all_to_all x2, starting transfers between devices, bring_back(): lax.all_to_all(values.reshape(experts, capacity, width).astype(jnp.bfloat...  7.65 us
    gather x3, local copies, waits for them, and re-layouts, bring_back(): picked = back.reshape(experts * capacity, width)[dest]  7 us
  transfers between devices with their start and end apart: 10, of which 4 were waited for; matrix products, arithmetic and copies ran while one was open for 23% of the time, Pallas kernels for 0%

commit v1 on v0

--- a/solution.py
+++ b/solution.py
@@ -126,7 +126,9 @@
     d_share, unused_dots = bring_back(d_rows, dest, jnp.ones_like(gates), experts, capacity, None)
     d_normed = d_share.T
     gain_local = jnp.sum(d_normed * mixed_f * scale[None, :], axis=1)
-    norm_terms = lax.psum(jnp.sum(d_normed * gain_f[:, None] * mixed_f, axis=0), "exp")
+    part_2 = jnp.sum(d_normed * gain_f[:, None] * mixed_f, axis=0)
+    terms = lax.all_gather(part_2, "exp", axis=0, tiled=False)
+    norm_terms = terms.sum(axis=0)
     cot_own = grad_out.astype(jnp.float32)
     d_mixed = (
         cot_own

time: 215 us -> 205 us (0.953)
  waiting for transfers between devices: 32.6 us -> 15.6 us
  blocking collectives: 81.2 us -> 88.7 us
    reduce_scatter x2, waiting for transfers between devices: 21.3 us -> 4.33 us  [bring_back(): lax.psum_scatter(term.astype(jnp.bfloat16), 'exp', scatter_dimension=1, t...]
    all_gather x0 -> x1, blocking collectives: none -> 7.91 us  [local(): terms = lax.all_gather(part_2, 'exp', axis=0, tiled=False)]
  transfers between devices with their start and end apart: 10 -> 10, of which waited for: 4 -> 3; matrix products, arithmetic and copies ran while one was open for 23% -> 25% of each run, Pallas kernels for 0% -> 0%
where the time goes in v1:
time: 205 us; the launch traced here: 204 us
  blocking collectives  88.7 us (43%)
  local copies, waits for them, and re-layouts  24.1 us (12%)
  starting transfers between devices  22.3 us (11%)
  matrix products  20.8 us (10%)
  other arithmetic  17.6 us (9%)
  waiting for transfers between devices  15.6 us (8%)
  between operations  15.1 us (7%)
    psum x1, blocking collectives, local(): grad_taps, grad_gain = lax.psum((tap_local, gain_local), 'ctx')  23.4 us
    psum x1, blocking collectives, local(): grad_gates = lax.psum(gate_dots, 'exp').reshape(tokens, 2)  16.6 us
    all_gather x1, blocking collectives, local(): lax.all_gather(grad_out, 'exp', axis=0, tiled=True)  15 us
    all_gather x1, blocking collectives, local(): lax.all_gather(normed_part, 'exp', axis=0, tiled=True)  13.8 us
    psum x1, blocking collectives, local(): squares = lax.psum(jnp.sum(mixed_f * mixed_f, axis=0), 'exp')  11.9 us
    all_gather x1, blocking collectives, local(): terms = lax.all_gather(part_2, 'exp', axis=0, tiled=False)  7.91 us
    all_to_all x2, starting transfers between devices, bring_back(): lax.all_to_all(values.reshape(experts, capacity, width).astype(jnp.bfloat...  7.65 us
    gather x3, local copies, waits for them, and re-layouts, bring_back(): picked = back.reshape(experts * capacity, width)[dest]  7 us
  transfers between devices with their start and end apart: 10, of which 3 were waited for; matrix products, arithmetic and copies ran while one was open for 25% of the time, Pallas kernels for 0%

profile of v1, /device:TPU:0, one launch (start us, length us, event | category | flops | bytes accessed | tf_op | source)
XLA Modules:
  0.0 204.2 jit_solution(6581926046643008269)
XLA Ops:
  8.8 2.9 %collective-permute-start.1 = (bf16[256,15]{0,1:T(8,128)(2,1)S(1)}, bf16[256,15]{0,1:T(8,128)(2,1)S(1)}, u32[]{:S(2)}, u32[]{:S(2)}) collective-permute-start(bf16[256,15]{0,1:T(8,128)(2,1)S(1)} %get-tuple-element.70), channel_id=1, source_target_pairs={{4,0},{8,4},{12,8},{16,12},{20,16},{24,20},{28,24},{0,28},{5,1},{9... | collective-permute-start | bytes 23048 | tf_op jit(solution)/shard_map/ppermute | solution.py:18
  15.5 15.0 %all_gather.13 = bf16[1024,128]{1,0:T(8,128)(2,1)S(1)} all-gather(bf16[256,128]{1,0:T(8,128)(2,1)} %param.17), channel_id=1, replica_groups=mesh['ctx'=8,'exp'=4] {'exp'}, dimensions={0}, use_global_device_ids=true | all-gather | bytes 327680 | tf_op jit(solution)/shard_map/all_gather | solution.py:79
  34.2 2.5 %scatter_custom_fusion.1 = bf16[256,1024]{1,0:T(8,128)(2,1)} fusion(s32[256]{0:T(256)S(1)} %bitcast.246, f32[256,1024]{1,0:T(8,128)S(1)} %convert_element_type.108, f32[256]{0:T(256)S(1)} %mul.828, bf16[]{:T(256)} %constant.8.clone.1), kind=kCustom, calls=%fused_computation.29 | custom fusion | flops 524288 | bytes 1573890 | tf_op jit(solution)/shard_map/scatter | solution.py:88
  36.7 4.1 %all-to-all-start.2 = ((bf16[8,32,1024]{2,1,0:T(8,128)(2,1)}), bf16[8,32,1024]{2,1,0:T(8,128)(2,1)}, u32[]{:S(2)}, u32[]{:S(2)}) async-start(bf16[8,32,1024]{2,1,0:T(8,128)(2,1)} %bitcast.150), calls=%async_computation.3 | async-start | bytes 1048576 | tf_op jit(solution)/shard_map/all_to_all | solution.py:91
  42.4 11.9 %psum.28 = f32[128]{0:T(128)S(1)} all-reduce(f32[128]{0:T(128)} %get-tuple-element.60), channel_id=1, replica_groups=mesh['ctx'=8,'exp'=4] {'exp'}, use_global_device_ids=true, to_apply=%region_4.5 | all-reduce | flops 128 | bytes 1024 | tf_op jit(solution)/shard_map/psum | solution.py:74
  54.9 13.8 %all_gather.12 = bf16[1024,128]{0,1:T(8,128)(2,1)S(1)} all-gather(bf16[256,128]{0,1:T(8,128)(2,1)S(1)} %fusion.27), channel_id=1, replica_groups=mesh['ctx'=8,'exp'=4] {'exp'}, dimensions={0}, use_global_device_ids=true | all-gather | bytes 327680 | tf_op jit(solution)/shard_map/all_gather | solution.py:78
  69.2 2.6 %scatter_custom_fusion = bf16[256,1024]{1,0:T(8,128)(2,1)} fusion(s32[256]{0:T(256)} %bitcast.247, bf16[256,1024]{1,0:T(8,128)(2,1)S(1)} %reshape.158, bf16[]{:T(256)} %constant.8.clone.1), kind=kCustom, calls=%fused_computation.41 | custom fusion | bytes 524800 | tf_op jit(solution)/shard_map/scatter | solution.py:87
  71.8 4.1 %all-to-all-start = ((bf16[8,32,1024]{2,1,0:T(8,128)(2,1)}), bf16[8,32,1024]{2,1,0:T(8,128)(2,1)S(1)}, u32[]{:S(2)}, u32[]{:S(2)}) async-start(bf16[8,32,1024]{2,1,0:T(8,128)(2,1)} %bitcast.36), calls=%async_computation | async-start | bytes 1048576 | tf_op jit(solution)/shard_map/all_to_all | solution.py:90
  76.5 3.5 %fusion.2 = f32[256,1024]{1,0:T(8,128)} fusion(bf16[256,1024]{1,0:T(8,128)(2,1)} %bitcast.47, bf16[1,1024,1024]{2,1,0:T(8,128)(2,1)} %param.16), kind=kOutput, calls=%fused_computation.6 | convolution fusion | flops 536870912 | bytes 3670016 | tf_op jit(solution)/shard_map/dot_general | solution.py:108
  80.0 5.6 %all-to-all-done = bf16[8,32,1024]{2,1,0:T(8,128)(2,1)S(1)} async-done(((bf16[8,32,1024]{2,1,0:T(8,128)(2,1)}), bf16[8,32,1024]{2,1,0:T(8,128)(2,1)S(1)}, u32[]{:S(2)}, u32[]{:S(2)}) %all-to-all-start) | async-done | bytes 524320 | tf_op jit(solution)/shard_map/all_to_all | solution.py:90
  85.6 2.5 %fusion.6 = f32[256,1024]{1,0:T(8,128)S(1)} fusion(bf16[256,1024]{1,0:T(8,128)(2,1)S(1)} %bitcast.146, bf16[1,1024,1024]{2,1,0:T(8,128)(2,1)} %param.15), kind=kOutput, calls=%fused_computation.10 | convolution fusion | flops 536870912 | bytes 3670016 | tf_op jit(solution)/shard_map/dot_general | solution.py:99
  92.5 3.5 %all-to-all-start.1 = ((bf16[8,32,1024]{2,1,0:T(8,128)(2,1)}), bf16[8,32,1024]{2,1,0:T(8,128)(2,1)S(1)}, u32[]{:S(2)}, u32[]{:S(2)}) async-start(bf16[8,32,1024]{2,1,0:T(8,128)(2,1)} %fusion.15), calls=%async_computation.1 | async-start | bytes 1048576 | tf_op jit(solution)/shard_map/all_to_all | solution.py:43
  100.0 5.7 %all-to-all-done.1 = bf16[8,32,1024]{2,1,0:T(8,128)(2,1)S(1)} async-done(((bf16[8,32,1024]{2,1,0:T(8,128)(2,1)}), bf16[8,32,1024]{2,1,0:T(8,128)(2,1)S(1)}, u32[]{:S(2)}, u32[]{:S(2)}) %all-to-all-start.1) | async-done | bytes 524320 | tf_op jit(solution)/shard_map/all_to_all | solution.py:43
  105.6 4.2 %all-to-all-start.3 = ((bf16[8,32,1024]{2,1,0:T(8,128)(2,1)}), bf16[8,32,1024]{2,1,0:T(8,128)(2,1)}, u32[]{:S(2)}, u32[]{:S(2)}) async-start(bf16[8,32,1024]{2,1,0:T(8,128)(2,1)} %bitcast.48), calls=%async_computation.4 | async-start | bytes 1048576 | tf_op jit(solution)/shard_map/all_to_all | solution.py:43
  113.3 2.9 %gather.9 = f32[128,2,1024]{2,1,0:T(2,128)} reshape(f32[256,1024]{1,0:T(8,128)} %gather_fusion) | data formatting | bytes 2097152 | tf_op jit(solution)/shard_map/gather | solution.py:50
  116.2 3.3 %multiply_reduce_fusion.1 = bf16[128,1024]{1,0:T(8,128)(2,1)} fusion(f32[128,2,1024]{2,1,0:T(2,128)} %gather.9, f32[128,2]{1,0:T(8,128)S(1)} %copy.35), kind=kLoop, calls=%fused_computation.26 | loop fusion | flops 393216 | bytes 1311744 | tf_op jit(solution)/shard_map/reduce_sum | solution.py:51
  125.0 2.9 %reshape.132 = f32[128,2,1024]{2,1,0:T(2,128)} reshape(f32[256,1024]{1,0:T(8,128)} %gather_fusion.1) | data formatting | bytes 2097152 | tf_op jit(solution)/shard_map/reshape | solution.py:51
  127.9 3.2 %reduce_sum.357 = bf16[128,1024]{1,0:T(8,128)(2,1)} reduce(f32[128,2,1024]{2,1,0:T(2,128)} %reshape.132, f32[]{:T(128)} %constant.7.clone.1), dimensions={1}, to_apply=%region_9.10 | reduce | flops 131072 | bytes 1310724 | tf_op jit(solution)/shard_map/reduce_sum | solution.py:51
  133.2 3.3 %convert_bitcast_fusion = bf16[1,1024,1024]{2,1,0:T(8,128)(2,1)} fusion(bf16[256,1024]{1,0:T(8,128)(2,1)S(1)} %copy-done.15, bf16[256,1024]{1,0:T(8,128)(2,1)} %bitcast.47), kind=kOutput, calls=%fused_computation.16 | convolution fusion | flops 537919488 | bytes 3145728 | tf_op jit(solution)/shard_map/dot_general | solution.py:111
  136.8 16.6 %psum.31 = f32[128,2]{1,0:T(8,128)S(1)} all-reduce(f32[128,2]{1,0:T(8,128)S(1)} %reshape.133), channel_id=1, replica_groups=mesh['ctx'=8,'exp'=4] {'exp'}, use_global_device_ids=true, to_apply=%region_48.49 | all-reduce | flops 256 | bytes 2048 | tf_op jit(solution)/shard_map/psum | solution.py:105
  154.1 4.3 %reduce-scatter.5.cloned.1.call-done = bf16[128,256]{1,0:T(8,128)(2,1)} async-done(((bf16[128,1024]{1,0:T(8,128)(2,1)}), bf16[128,256]{1,0:T(8,128)(2,1)}) %reduce-scatter.5.cloned.1.call-update) | async-done | bytes 65552 | tf_op jit(solution)/shard_map/reduce_scatter | solution.py:52
  159.4 7.9 %all-gather.1 = f32[4,1,128]{2,1,0:T(1,128)S(1)} all-gather(f32[1,1,128]{2,1,0:T(1,128)S(1)} %bitcast.250), channel_id=2, replica_groups=mesh['ctx'=8,'exp'=4] {'exp'}, dimensions={0}, use_global_device_ids=true | all-gather | bytes 2560 | tf_op jit(solution)/shard_map/all_gather | solution.py:130
  169.1 2.6 %collective-permute-start.3 = (bf16[256,15]{0,1:T(8,128)(2,1)S(1)}, bf16[256,15]{0,1:T(8,128)(2,1)S(1)}, u32[]{:S(2)}, u32[]{:S(2)}) collective-permute-start(bf16[256,15]{0,1:T(8,128)(2,1)S(1)} %get-tuple-element.67), channel_id=1, source_target_pairs={{4,0},{8,4},{12,8},{16,12},{20,16},{24,20},{28,24},{0,28},{5,1},{9... | collective-permute-start | bytes 23048 | tf_op jit(solution)/shard_map/ppermute | solution.py:18
  171.8 23.4 %all-reduce = (f32[256,31]{0,1:T(8,128)}, f32[256]{0:T(256)}) all-reduce(f32[256,31]{0,1:T(8,128)S(1)} %stack.127, f32[256]{0:T(256)S(1)} %get-tuple-element.55), channel_id=1, replica_groups=mesh['ctx'=8,'exp'=4] {'ctx'}, use_global_device_ids=true, to_apply=%region_44.45 | all-reduce | flops 8192 | bytes 65536 | tf_op jit(solution)/shard_map/psum | solution.py:149
  (201 shorter events, 36.7 us)
Async XLA Ops:
  7.2 81.0 %copy-start = (bf16[1,1024,1024]{2,1,0:T(8,128)(2,1)S(1)}, bf16[1,1024,1024]{2,1,0:T(8,128)(2,1)}, u32[]{:S(2)}) copy-start(bf16[1,1024,1024]{2,1,0:T(8,128)(2,1)} %param.14) | copy-start | bytes 6291460
  8.3 32.8 %collective-permute-start = (bf16[256,15]{0,1:T(8,128)(2,1)S(1)}, bf16[256,15]{0,1:T(8,128)(2,1)S(1)}, u32[]{:S(2)}, u32[]{:S(2)}) collective-permute-start(bf16[256,15]{0,1:T(8,128)(2,1)S(1)} %get-tuple-element.69), channel_id=1, source_target_pairs={{0,4},{4,8},{8,12},{12,16},{16,20},{20,24},{24,28},{28,0},{1,5},{5... | collective-permute-start | bytes 23048 | tf_op jit(solution)/shard_map/ppermute | solution.py:16
  8.8 32.4 %collective-permute-start.1 = (bf16[256,15]{0,1:T(8,128)(2,1)S(1)}, bf16[256,15]{0,1:T(8,128)(2,1)S(1)}, u32[]{:S(2)}, u32[]{:S(2)}) collective-permute-start(bf16[256,15]{0,1:T(8,128)(2,1)S(1)} %get-tuple-element.70), channel_id=1, source_target_pairs={{4,0},{8,4},{12,8},{16,12},{20,16},{24,20},{28,24},{0,28},{5,1},{9... | collective-permute-start | bytes 23048 | tf_op jit(solution)/shard_map/ppermute | solution.py:18
  36.7 35.1 %all-to-all-start.2 = ((bf16[8,32,1024]{2,1,0:T(8,128)(2,1)}), bf16[8,32,1024]{2,1,0:T(8,128)(2,1)}, u32[]{:S(2)}, u32[]{:S(2)}) async-start(bf16[8,32,1024]{2,1,0:T(8,128)(2,1)} %bitcast.150), calls=%async_computation.3 | async-start | bytes 1048576 | tf_op jit(solution)/shard_map/all_to_all | solution.py:91
  71.8 13.8 %all-to-all-start = ((bf16[8,32,1024]{2,1,0:T(8,128)(2,1)}), bf16[8,32,1024]{2,1,0:T(8,128)(2,1)S(1)}, u32[]{:S(2)}, u32[]{:S(2)}) async-start(bf16[8,32,1024]{2,1,0:T(8,128)(2,1)} %bitcast.36), calls=%async_computation | async-start | bytes 1048576 | tf_op jit(solution)/shard_map/all_to_all | solution.py:90
  92.5 13.2 %all-to-all-start.1 = ((bf16[8,32,1024]{2,1,0:T(8,128)(2,1)}), bf16[8,32,1024]{2,1,0:T(8,128)(2,1)S(1)}, u32[]{:S(2)}, u32[]{:S(2)}) async-start(bf16[8,32,1024]{2,1,0:T(8,128)(2,1)} %fusion.15), calls=%async_computation.1 | async-start | bytes 1048576 | tf_op jit(solution)/shard_map/all_to_all | solution.py:43
  105.6 16.2 %all-to-all-start.3 = ((bf16[8,32,1024]{2,1,0:T(8,128)(2,1)}), bf16[8,32,1024]{2,1,0:T(8,128)(2,1)}, u32[]{:S(2)}, u32[]{:S(2)}) async-start(bf16[8,32,1024]{2,1,0:T(8,128)(2,1)} %bitcast.48), calls=%async_computation.4 | async-start | bytes 1048576 | tf_op jit(solution)/shard_map/all_to_all | solution.py:43
  109.8 44.3 %reduce-scatter.3.cloned.1.call-start = ((), (), s32[]{:S(2)}) async-start(), calls=%async_computation.6 | async-start | bytes 327680 | tf_op jit(solution)/shard_map/reduce_scatter | solution.py:52
  119.6 38.8 %reduce-scatter.5.cloned.1.call-start = ((), (), s32[]{:S(2)}) async-start(), calls=%async_computation.7 | async-start | bytes 327680 | tf_op jit(solution)/shard_map/reduce_scatter | solution.py:52
  136.5 30.9 %copy-start.65 = (f32[128]{0:T(128)S(1)}, f32[128]{0:T(128)}, u32[]{:S(2)}) copy-start(f32[128]{0:T(128)} %copy-done.64) | copy-start | bytes 1540
  167.4 28.7 %copy-start.19 = (f32[256,1]{0,1:T(1,128)S(1)}, f32[256,1]{0,1:T(1,128)}, u32[]{:S(2)}) copy-start(f32[256,1]{0,1:T(1,128)} %copy-done.18) | copy-start | bytes 3076
  167.4 28.7 %copy-start.21 = (f32[256,1]{0,1:T(1,128)S(1)}, f32[256,1]{0,1:T(1,128)}, u32[]{:S(2)}) copy-start(f32[256,1]{0,1:T(1,128)} %copy-done.20) | copy-start | bytes 3076
  167.4 28.7 %copy-start.23 = (f32[256,1]{0,1:T(1,128)S(1)}, f32[256,1]{0,1:T(1,128)}, u32[]{:S(2)}) copy-start(f32[256,1]{0,1:T(1,128)} %copy-done.22) | copy-start | bytes 3076
  167.4 28.7 %copy-start.25 = (f32[256,1]{0,1:T(1,128)S(1)}, f32[256,1]{0,1:T(1,128)}, u32[]{:S(2)}) copy-start(f32[256,1]{0,1:T(1,128)} %copy-done.24) | copy-start | bytes 3076
  167.4 28.7 %copy-start.27 = (f32[256,1]{0,1:T(1,128)S(1)}, f32[256,1]{0,1:T(1,128)}, u32[]{:S(2)}) copy-start(f32[256,1]{0,1:T(1,128)} %copy-done.26) | copy-start | bytes 3076
  167.4 28.7 %copy-start.29 = (f32[256,1]{0,1:T(1,128)S(1)}, f32[256,1]{0,1:T(1,128)}, u32[]{:S(2)}) copy-start(f32[256,1]{0,1:T(1,128)} %copy-done.28) | copy-start | bytes 3076
  167.4 28.7 %copy-start.31 = (f32[256,1]{0,1:T(1,128)S(1)}, f32[256,1]{0,1:T(1,128)}, u32[]{:S(2)}) copy-start(f32[256,1]{0,1:T(1,128)} %copy-done.30) | copy-start | bytes 3076
  167.4 28.7 %copy-start.33 = (f32[256,1]{0,1:T(1,128)S(1)}, f32[256,1]{0,1:T(1,128)}, u32[]{:S(2)}) copy-start(f32[256,1]{0,1:T(1,128)} %copy-done.32) | copy-start | bytes 3076
  167.4 28.7 %copy-start.35 = (f32[256,1]{0,1:T(1,128)S(1)}, f32[256,1]{0,1:T(1,128)}, u32[]{:S(2)}) copy-start(f32[256,1]{0,1:T(1,128)} %copy-done.34) | copy-start | bytes 3076
  167.4 28.7 %copy-start.37 = (f32[256,1]{0,1:T(1,128)S(1)}, f32[256,1]{0,1:T(1,128)}, u32[]{:S(2)}) copy-start(f32[256,1]{0,1:T(1,128)} %copy-done.36) | copy-start | bytes 3076
  167.5 28.7 %copy-start.39 = (f32[256,1]{0,1:T(1,128)S(1)}, f32[256,1]{0,1:T(1,128)}, u32[]{:S(2)}) copy-start(f32[256,1]{0,1:T(1,128)} %copy-done.38) | copy-start | bytes 3076
  167.5 28.7 %copy-start.41 = (f32[256,1]{0,1:T(1,128)S(1)}, f32[256,1]{0,1:T(1,128)}, u32[]{:S(2)}) copy-start(f32[256,1]{0,1:T(1,128)} %copy-done.40) | copy-start | bytes 3076
  169.0 27.0 %collective-permute-start.2 = (bf16[256,15]{0,1:T(8,128)(2,1)S(1)}, bf16[256,15]{0,1:T(8,128)(2,1)S(1)}, u32[]{:S(2)}, u32[]{:S(2)}) collective-permute-start(bf16[256,15]{0,1:T(8,128)(2,1)S(1)} %get-tuple-element.66), channel_id=1, source_target_pairs={{0,4},{4,8},{8,12},{12,16},{16,20},{20,24},{24,28},{28,0},{1,5},{5... | collective-permute-start | bytes 23048 | tf_op jit(solution)/shard_map/ppermute | solution.py:16
  169.1 26.9 %collective-permute-start.3 = (bf16[256,15]{0,1:T(8,128)(2,1)S(1)}, bf16[256,15]{0,1:T(8,128)(2,1)S(1)}, u32[]{:S(2)}, u32[]{:S(2)}) collective-permute-start(bf16[256,15]{0,1:T(8,128)(2,1)S(1)} %get-tuple-element.67), channel_id=1, source_target_pairs={{4,0},{8,4},{12,8},{16,12},{20,16},{24,20},{28,24},{0,28},{5,1},{9... | collective-permute-start | bytes 23048 | tf_op jit(solution)/shard_map/ppermute | solution.py:18
  (52 other events, 423.0 us)
Sparse Core Ops, SparseCore 0:
  119.7 18.0 reduce-scatter.2
  140.1 18.2 reduce-scatter.4
